TPU v7x, 32 devices: a whole 2x2x4 slice. The times are simulated.
32 devices in a mesh: row: 4 (over z), col: 8 (over y, x, core).
Axes of the slice: x: 2, y: 2, z: 4, core: 2. Of those that a mesh axis runs over, the one named last changes fastest.
Arguments:
- blocks: bfloat16 [2048, 128, 128], P(('row', 'col'))
- owners: int32 [2048], P(('row', 'col')), may hold values from 0 to 7, as said below
- places: int32 [2048], P(('row', 'col')), may hold values from 0 to 127, as said below
- panel_matrix: bfloat16 [64, 128, 512], P('col', 'row'), may hold values from -6 to 6
Outputs:
- inflated: float32 [8192, 512], P(('row', 'col'))
Inputs may be any that keep to these rules, and one draw needn't show every extreme that they name: `owners`: on each device at most 16 slots name the same owner; for each index of row one owner is named by exactly 16 slots of every device with that row index. `places`: two slots on devices of the same row index that name the same owner never have the same place.
All inputs are finite; a program needn't handle non-finite values.
Results may differ from a plain program's by a relative error of at most 0.0003.
Values may be sent and summed in bfloat16 or wider, within the bound.
A program may use at most 128 MiB of HBM per device.

v0:
```python
import jax
import jax.numpy as jnp
from jax import lax
from jax.sharding import PartitionSpec as P

epsilon = 1e-06


def on_device(blocks, owners, places, panel_matrix):
    col_count = lax.axis_size("col")
    row_count = lax.axis_size("row")
    col_blocks = panel_matrix.shape[0]
    block_side = blocks.shape[1]
    panel_width = panel_matrix.shape[2]
    row_blocks = col_blocks * col_count // row_count
    capacity = row_blocks * col_blocks // col_count
    targets = jnp.arange(col_count, dtype=jnp.int32)
    onehot = (owners[:, None] == targets[None, :]).astype(jnp.int32)
    before = jnp.cumsum(onehot, axis=0) - onehot
    bucket_rank = jnp.sum(before * onehot, axis=1)
    slot_index = owners * capacity + bucket_rank
    received = col_count * capacity
    outgoing = (
        jnp.zeros((received, block_side, block_side), blocks.dtype).at[slot_index].set(blocks)
    )
    out_places = jnp.zeros((received,), jnp.int32).at[slot_index].set(places)
    outgoing = outgoing.reshape(col_count, capacity, block_side, block_side)
    out_places = out_places.reshape(col_count, capacity)
    arrived, arrived_places = (
        lax.all_to_all(outgoing, "col", split_axis=0, concat_axis=0, tiled=True),
        lax.all_to_all(out_places, "col", split_axis=0, concat_axis=0, tiled=True),
    )
    arrived = arrived.reshape(received, block_side, block_side)
    arrived_places = arrived_places.reshape(received)
    row_in = arrived_places // col_blocks
    col_in = arrived_places % col_blocks
    panel_full = lax.all_gather(panel_matrix, "row", axis=1, tiled=True)
    group_size = min(32, received)
    turn_count = received // group_size

    def add_group(partial_value, members):
        tile_group, group_rows, group_cols = members
        pieces = panel_full[group_cols]
        product = jnp.einsum("sab,sbp->sap", tile_group, pieces, preferred_element_type=jnp.float32)
        return (partial_value.at[group_rows].add(product), None)

    start_sum = jnp.zeros((row_blocks, block_side, panel_width), jnp.float32)
    partial_value = lax.scan(
        add_group,
        start_sum,
        (
            arrived.reshape(turn_count, group_size, block_side, block_side),
            row_in.reshape(turn_count, group_size),
            col_in.reshape(turn_count, group_size),
        ),
    )[0]
    partial_rows = partial_value.reshape(row_blocks * block_side, panel_width)
    own_rows = lax.psum_scatter(partial_rows, "col", scatter_dimension=0, tiled=True)
    squares = own_rows * own_rows
    totals = lax.psum(jnp.sum(squares, axis=0), ("row", "col"))
    col_mean = totals / (col_blocks * col_count * block_side)
    return squares / (col_mean + epsilon)


def solution(mesh):
    placed = (
        P(("row", "col"), None, None),
        P(("row", "col")),
        P(("row", "col")),
        P("col", "row", None),
    )
    return jax.shard_map(
        on_device, mesh=mesh, in_specs=placed, out_specs=P(("row", "col"), None), check_vma=False
    )
```

profile of v0, /device:TPU:0, one launch (start us, length us, event | category | flops | bytes accessed | tf_op | source)
XLA Modules:
  0.0 296.1 jit_solution(16215350715262067872)
XLA Ops:
  10.6 5.2 %all-to-all-start = ((s32[8,1,16]{2,1,0:T(1,128)}), s32[8,1,16]{2,1,0:T(1,128)S(1)}, u32[]{:S(2)}, u32[]{:S(2)}) async-start(s32[8,1,16]{2,1,0:T(1,128)} %bitcast.5), calls=%async_computation | async-start | bytes 8192 | tf_op jit(solution)/shard_map/all_to_all | solution.py:31
  15.8 3.0 %broadcast_in_dim.21 = bf16[128,128,128]{2,1,0:T(8,128)(2,1)} broadcast(bf16[]{:T(256)} %constant.54.clone.1), dimensions={} | broadcast | bytes 4194306 | tf_op jit(solution)/shard_map/broadcast_in_dim | solution.py:24
  18.7 8.6 %scatter_fusion.1 = bf16[128,128,128]{2,1,0:T(8,128)(2,1)} fusion(bf16[128,128,128]{2,1,0:T(8,128)(2,1)} %broadcast_in_dim.21, s32[64]{0:T(128)S(1)} %compare_select_fusion.2, bf16[64,128,128]{2,1,0:T(8,128)(2,1)S(1)} %copy-done.1), kind=kCustom, calls=%fused_computation.3 | custom fusion | bytes 6291712 | tf_op jit(solution)/shard_map/scatter | solution.py:24
  27.4 4.6 %all-to-all-start.1 = ((bf16[8,16,128,128]{3,2,1,0:T(8,128)(2,1)}), bf16[8,16,128,128]{3,2,1,0:T(8,128)(2,1)}, u32[]{:S(2)}, u32[]{:S(2)}) async-start(bf16[8,16,128,128]{3,2,1,0:T(8,128)(2,1)} %bitcast.33), calls=%async_computation.1 | async-start | bytes 8388608 | tf_op jit(solution)/shard_map/all_to_all | solution.py:30
  34.0 30.0 %all-gather.2.cloned.1.call-done = bf16[8,128,512]{2,1,0:T(8,128)(2,1)} async-done(((bf16[8,32,512]{2,1,0:T(8,128)(2,1)}), bf16[8,128,512]{2,1,0:T(8,128)(2,1)}) %all-gather.2.cloned.1.call-update) | async-done | bytes 1048592 | tf_op jit(solution)/shard_map/all_gather | solution.py:37
  64.0 17.1 %all-to-all-done.1 = bf16[8,16,128,128]{3,2,1,0:T(8,128)(2,1)} async-done(((bf16[8,16,128,128]{3,2,1,0:T(8,128)(2,1)}), bf16[8,16,128,128]{3,2,1,0:T(8,128)(2,1)}, u32[]{:S(2)}, u32[]{:S(2)}) %all-to-all-start.1) | async-done | bytes 4194336 | tf_op jit(solution)/shard_map/all_to_all | solution.py:30
  81.1 2.5 broadcast_in_dim.8
  83.6 111.2 %while.10 = (s32[]{:T(128)}, f32[16,128,512]{2,1,0:T(8,128)}, s32[4,32]{1,0:T(4,128)S(1)}, bf16[4,32,128,128]{3,2,1,0:T(8,128)(2,1)}, s32[4,32]{1,0:T(4,128)S(1)}, /*index=5*/bf16[8,128,512]{2,1,0:T(8,128)(2,1)S(1)}, s32[]{:T(128)}) while((s32[]{:T(128)}, f32[16,128,512]{2,1,0:T(8,128)}, s32[4,32]{1,0:T(4,128)S(1)}, ...), condition=%wide.region_6.7_spmd, body=%wide.region_4.6_spmd.sunk | while | flops 538969280 | bytes 47191504 | solution.py:48
  83.6 2.7 gather_fusion
  86.4 7.0 %fusion.20 = f32[32,128,512]{2,1,0:T(8,128)} fusion(bf16[32,128,512]{2,1,0:T(8,128)(2,1)} %gather_fusion, bf16[4,32,128,128]{3,2,1,0:T(8,128)(2,1)} %get-tuple-element.112, s32[]{:T(128)} %get-tuple-element.102), kind=kOutput, calls=%fused_computation.4.clone.1 | convolution fusion | flops 536870912 | bytes 13632000 | tf_op jit(solution)/shard_map/while/body/eval_jaxpr/sab,sbp->sap/dot_general | solution.py:44
  93.3 18.1 %scatter_fusion = f32[16,128,512]{2,1,0:T(8,128)} fusion(f32[16,128,512]{2,1,0:T(8,128)} %get-tuple-element.103, s32[32]{0:T(128)S(1)} %get-tuple-element.93, f32[32,128,512]{2,1,0:T(8,128)} %fusion.20), kind=kCustom, calls=%fused_computation.1.clone.1 | custom fusion | flops 2097152 | bytes 25165952 | tf_op jit(solution)/shard_map/while/body/eval_jaxpr/scatter-add | solution.py:45
  111.4 2.7 gather_fusion
  114.2 7.0 %fusion.20 = f32[32,128,512]{2,1,0:T(8,128)} fusion(bf16[32,128,512]{2,1,0:T(8,128)(2,1)} %gather_fusion, bf16[4,32,128,128]{3,2,1,0:T(8,128)(2,1)} %get-tuple-element.112, s32[]{:T(128)} %get-tuple-element.102), kind=kOutput, calls=%fused_computation.4.clone.1 | convolution fusion | flops 536870912 | bytes 13632000 | tf_op jit(solution)/shard_map/while/body/eval_jaxpr/sab,sbp->sap/dot_general | solution.py:44
  121.1 18.1 %scatter_fusion = f32[16,128,512]{2,1,0:T(8,128)} fusion(f32[16,128,512]{2,1,0:T(8,128)} %get-tuple-element.103, s32[32]{0:T(128)S(1)} %get-tuple-element.93, f32[32,128,512]{2,1,0:T(8,128)} %fusion.20), kind=kCustom, calls=%fused_computation.1.clone.1 | custom fusion | flops 2097152 | bytes 25165952 | tf_op jit(solution)/shard_map/while/body/eval_jaxpr/scatter-add | solution.py:45
  139.2 2.7 gather_fusion
  142.0 7.0 %fusion.20 = f32[32,128,512]{2,1,0:T(8,128)} fusion(bf16[32,128,512]{2,1,0:T(8,128)(2,1)} %gather_fusion, bf16[4,32,128,128]{3,2,1,0:T(8,128)(2,1)} %get-tuple-element.112, s32[]{:T(128)} %get-tuple-element.102), kind=kOutput, calls=%fused_computation.4.clone.1 | convolution fusion | flops 536870912 | bytes 13632000 | tf_op jit(solution)/shard_map/while/body/eval_jaxpr/sab,sbp->sap/dot_general | solution.py:44
  148.9 18.1 %scatter_fusion = f32[16,128,512]{2,1,0:T(8,128)} fusion(f32[16,128,512]{2,1,0:T(8,128)} %get-tuple-element.103, s32[32]{0:T(128)S(1)} %get-tuple-element.93, f32[32,128,512]{2,1,0:T(8,128)} %fusion.20), kind=kCustom, calls=%fused_computation.1.clone.1 | custom fusion | flops 2097152 | bytes 25165952 | tf_op jit(solution)/shard_map/while/body/eval_jaxpr/scatter-add | solution.py:45
  167.0 2.7 gather_fusion
  169.8 7.0 %fusion.20 = f32[32,128,512]{2,1,0:T(8,128)} fusion(bf16[32,128,512]{2,1,0:T(8,128)(2,1)} %gather_fusion, bf16[4,32,128,128]{3,2,1,0:T(8,128)(2,1)} %get-tuple-element.112, s32[]{:T(128)} %get-tuple-element.102), kind=kOutput, calls=%fused_computation.4.clone.1 | convolution fusion | flops 536870912 | bytes 13632000 | tf_op jit(solution)/shard_map/while/body/eval_jaxpr/sab,sbp->sap/dot_general | solution.py:44
  176.7 18.1 %scatter_fusion = f32[16,128,512]{2,1,0:T(8,128)} fusion(f32[16,128,512]{2,1,0:T(8,128)} %get-tuple-element.103, s32[32]{0:T(128)S(1)} %get-tuple-element.93, f32[32,128,512]{2,1,0:T(8,128)} %fusion.20), kind=kCustom, calls=%fused_computation.1.clone.1 | custom fusion | flops 2097152 | bytes 25165952 | tf_op jit(solution)/shard_map/while/body/eval_jaxpr/scatter-add | solution.py:45
  194.8 52.1 %reduce-scatter.2.cloned.1.call-done = f32[256,512]{1,0:T(8,128)} async-done(((f32[2048,512]{1,0:T(8,128)}), f32[256,512]{1,0:T(8,128)}) %reduce-scatter.2.cloned.1.call-update) | async-done | bytes 524304 | tf_op jit(solution)/shard_map/reduce_scatter | solution.py:58
  246.9 1.1 multiply_reduce_fusion
  248.0 39.3 %psum.7 = f32[512]{0:T(512)S(1)} all-reduce(f32[512]{0:T(512)S(1)} %multiply_reduce_fusion), channel_id=1, replica_groups=mesh['row'=4,'col'=8] {'row','col'}, use_global_device_ids=true, to_apply=%region_9.10 | all-reduce | flops 512 | bytes 4096 | tf_op jit(solution)/shard_map/psum | solution.py:60
  287.4 1.9 multiply_divide_fusion
  (28 shorter events, 6.2 us)
Async XLA Ops:
  6.5 12.2 %copy-start.1 = (bf16[64,128,128]{2,1,0:T(8,128)(2,1)S(1)}, bf16[64,128,128]{2,1,0:T(8,128)(2,1)}, u32[]{:S(2)}) copy-start(bf16[64,128,128]{2,1,0:T(8,128)(2,1)} %param.6) | copy-start | bytes 6291460
  10.6 16.8 %all-to-all-start = ((s32[8,1,16]{2,1,0:T(1,128)}), s32[8,1,16]{2,1,0:T(1,128)S(1)}, u32[]{:S(2)}, u32[]{:S(2)}) async-start(s32[8,1,16]{2,1,0:T(1,128)} %bitcast.5), calls=%async_computation | async-start | bytes 8192 | tf_op jit(solution)/shard_map/all_to_all | solution.py:31
  27.4 53.7 %all-to-all-start.1 = ((bf16[8,16,128,128]{3,2,1,0:T(8,128)(2,1)}), bf16[8,16,128,128]{3,2,1,0:T(8,128)(2,1)}, u32[]{:S(2)}, u32[]{:S(2)}) async-start(bf16[8,16,128,128]{3,2,1,0:T(8,128)(2,1)} %bitcast.33), calls=%async_computation.1 | async-start | bytes 8388608 | tf_op jit(solution)/shard_map/all_to_all | solution.py:30
  32.0 32.0 %all-gather.2.cloned.1.call-start = ((), (), s32[]{:S(2)}) async-start(), calls=%async_computation.3 | async-start | bytes 1310720 | tf_op jit(solution)/shard_map/all_gather | solution.py:37
  32.7 214.2 %reduce-scatter.2.cloned.1.call-start = ((), (), s32[]{:S(2)}) async-start(), calls=%async_computation.4 | async-start | bytes 4718592 | tf_op jit(solution)/shard_map/reduce_scatter | solution.py:58
  64.0 19.6 %copy-start = (bf16[8,128,512]{2,1,0:T(8,128)(2,1)S(1)}, bf16[8,128,512]{2,1,0:T(8,128)(2,1)}, u32[]{:S(2)}) copy-start(bf16[8,128,512]{2,1,0:T(8,128)(2,1)} %all-gather.2.cloned.1.call-done) | copy-start | bytes 3145732
Sparse Core Ops, SparseCore 0:
  34.4 29.5 all-gather.1
  194.9 51.9 reduce-scatter.1
where the time goes:
time: 297 us; the launch traced here: 296 us
  waiting for transfers between devices  99.9 us (34%)
  other arithmetic  78.5 us (26%)
  blocking collectives  39.3 us (13%)
  matrix products  27.9 us (9%)
  local copies, waits for them, and re-layouts  27.2 us (9%)
  between operations  13.4 us (5%)
  starting transfers between devices  9.85 us (3%)
    scatter-add x4, other arithmetic, add_group(): return (partial_value.at[group_rows].add(product), None)  72.3 us
    reduce_scatter x1, waiting for transfers between devices, on_device(): lax.psum_scatter(partial_rows, 'col', scatter_dimension=0, tiled=True)  52.1 us
    psum x1, blocking collectives, on_device(): totals = lax.psum(jnp.sum(squares, axis=0), ('row', 'col'))  39.3 us
    all_gather x1, waiting for transfers between devices, on_device(): panel_full = lax.all_gather(panel_matrix, 'row', axis=1, tiled=True)  30 us
    dot_general x4, matrix products, add_group(): jnp.einsum('sab,sbp->sap', tile_group, pieces, preferred_element_type=jnp...  27.9 us
    all_to_all x1, waiting for transfers between devices, on_device(): lax.all_to_all(outgoing, 'col', split_axis=0, concat_axis=0, tiled=True)  17.1 us
    gather x4, local copies, waits for them, and re-layouts, add_group(): pieces = panel_full[group_cols]  11 us
    scatter x1, local copies, waits for them, and re-layouts, on_device(): jnp.zeros((received, block_side, block_side), blocks.dtype).at[slot_index]  8.63 us
  transfers between devices with their start and end apart: 4, of which 3 were waited for; matrix products, arithmetic and copies ran while one was open for 4% of the time, Pallas kernels for 0%

commit v1 on v0

--- a/solution.py
+++ b/solution.py
@@ -1,9 +1,443 @@
+import functools
+
 import jax
 import jax.numpy as jnp
 from jax import lax
+from jax.experimental import pallas as pl
+from jax.experimental.pallas import tpu as pltpu
 from jax.sharding import PartitionSpec as P
 
 epsilon = 1e-06
+CHIPS = 4
+PARTS = 2
+UNROLL = 8
+MESH = pl.DeviceIdType.MESH
+
+
+def slot_table(owners, places, col_blocks, row_blocks):
+    count = owners.shape[0]
+    ids = jnp.arange(count, dtype=jnp.int32)
+    rows = places // col_blocks
+    cols = owners * col_blocks + places % col_blocks
+    key = rows * count + ids
+    rank = jnp.sum((key[None, :] < key[:, None]).astype(jnp.int32), axis=1)
+    chosen = (rank[None, :] == ids[:, None]).astype(jnp.int32)
+    code = jnp.sum(chosen * (cols * count + ids)[None, :], axis=1)
+    row_at = jnp.sum(chosen * rows[None, :], axis=1)
+    first = jnp.concatenate(
+        [jnp.ones((1,), jnp.int32), (row_at[1:] != row_at[:-1]).astype(jnp.int32)]
+    )
+    targets = jnp.arange(row_blocks, dtype=jnp.int32)
+    upto = jnp.sum((rows[None, :] <= targets[:, None]).astype(jnp.int32), axis=1)
+    some = jnp.any(rows[None, :] == targets[:, None], axis=1)
+    last = jnp.where(some, upto, 0)
+    lines = [jnp.pad(v, (0, 128 - v.shape[0])) for v in (code, first, last)]
+    return jnp.stack(lines + [jnp.zeros((128,), jnp.int32)] * 5)
+
+
+def panel_kernel(
+    cfg,
+    blocks_ref, table_ref, panel_ref,
+    squares_ref, totals_ref,
+    pan0, pan1, own_blocks, sib_blocks, own_table, sib_table, sib_table_vmem,
+    run, part0, part1, arrive0, arrive1, sib_in, sib_out, mine, stats,
+    local_sem, pair_send, pair_recv,
+    za_send, za_recv, zb_send, zb_recv,
+    xa_send, xa_recv, ra_send, ra_recv,
+    xb_send, xb_recv, rb_send, rb_recv,
+    rs_send, rs_recv, out_send, out_recv, st_send, st_recv,
+):
+    R, S, CB, RB, BS, width, n_a = cfg
+    C = 2 * CHIPS
+    slab_rows = BS // R
+    group = 2 * CB
+    quarter = RB // CHIPS
+    own_rows = quarter // 2
+    pans, parts, arrives = (pan0, pan1), (part0, part1), (arrive0, arrive1)
+    z = lax.axis_index("row")
+    c = lax.axis_index("col")
+    q = c // 2
+    k = c % 2
+    qx = q + 1 - 2 * (q % 2)
+    qy = lax.rem(q + 2, 4)
+    qd = 3 - q
+    me = z * C + c
+    total_devices = R * C
+    nbrs = (qx, qy)
+    sent = []
+
+    def true():
+        return None
+
+    def when(cond, f):
+        if cond is None:
+            f()
+        else:
+            pl.when(cond)(f)
+
+    def start(mk, cond=None):
+        when(cond, lambda: mk().start())
+        sent.append((mk, cond))
+
+    def remote(src, dst, s, r, dev):
+        return pltpu.make_async_remote_copy(
+            src_ref=src, dst_ref=dst, send_sem=s, recv_sem=r, device_id=dev, device_id_type=MESH
+        )
+
+    barrier = pltpu.get_barrier_semaphore()
+
+    def greet(d, carry):
+        t = lax.rem(me + d, total_devices)
+        pl.semaphore_signal(barrier, inc=1, device_id=(t // C, t % C), device_id_type=MESH)
+        return carry
+
+    lax.fori_loop(1, total_devices, greet, 0)
+
+    def slab(zz):
+        return pl.ds(pl.multiple_of(zz * slab_rows, slab_rows), slab_rows)
+
+    def local(i, src, dst):
+        return pltpu.make_async_copy(src, dst, local_sem.at[i])
+
+    def panel_cols(core, j):
+        return pl.ds(pl.multiple_of((core * PARTS + j) * width, width), width)
+
+    for j in range(PARTS):
+        local(
+            j, panel_ref.at[:, :, panel_cols(k, j)],
+            pans[j].at[q, pl.ds(k * CB, CB), slab(z)],
+        ).start()
+    local(2, table_ref, own_table).start()
+    local(3, blocks_ref, own_blocks).start()
+    pl.semaphore_wait(barrier, total_devices - 1)
+
+    sib = (z, q * 2 + 1 - k)
+
+    def pair_panel(j):
+        return remote(
+            panel_ref.at[:, :, panel_cols(1 - k, j)],
+            pans[j].at[q, pl.ds(k * CB, CB), slab(z)],
+            pair_send.at[j], pair_recv.at[j], sib,
+        )
+
+    for j in range(PARTS):
+        start(functools.partial(pair_panel, j))
+
+    def pair_table():
+        return remote(table_ref, sib_table_vmem, pair_send.at[2], pair_recv.at[2], sib)
+
+    def pair_blocks():
+        return remote(blocks_ref, sib_blocks, pair_send.at[3], pair_recv.at[3], sib)
+
+    start(pair_table)
+    start(pair_blocks)
+
+    def dev_q(qq):
+        return (z, qq * 2 + k)
+
+    def a_range(part):
+        half = n_a // 2
+        return (pl.ds(0, n_a), pl.ds(0, half), pl.ds(half, n_a - half))[part]
+
+    def b_range(part):
+        n_b = group - n_a
+        half = n_b // 2
+        return (pl.ds(n_a, n_b), pl.ds(n_a, half), pl.ds(n_a + half, n_b - half))[part]
+
+    def za(j, up, d):
+        shard = z - (d - 1) if up else z + (d - 1)
+        view = pans[j].at[q, a_range(0), slab(jnp.clip(shard, 0, R - 1))]
+        i = (j * 2 + up) * R + d - 1
+        to = jnp.clip(z + 1 if up else z - 1, 0, R - 1)
+        return remote(view, view, za_send.at[i], za_recv.at[i], (to, c))
+
+    def zb(j, up, d):
+        shard = z - (d - 1) if up else z + (d - 1)
+        view = pans[j].at[:, b_range(0), slab(jnp.clip(shard, 0, R - 1))]
+        i = (j * 2 + up) * R + d - 1
+        to = jnp.clip(z + 1 if up else z - 1, 0, R - 1)
+        return remote(view, view, zb_send.at[i], zb_recv.at[i], (to, c))
+
+    def z_send_cond(up, d):
+        if up:
+            return jnp.logical_and(z - (d - 1) >= 0, z + 1 < R)
+        return jnp.logical_and(z + (d - 1) < R, z - 1 >= 0)
+
+    def z_recv_cond(up, d):
+        return z - d >= 0 if up else z + d < R
+
+    def z_from(up, d):
+        return jnp.clip(z - d if up else z + d, 0, R - 1)
+
+    def xa(j, n, zz):
+        view = pans[j].at[q, a_range(0), slab(zz)]
+        i = (j * 2 + n) * R + zz
+        return remote(view, view, xa_send.at[i], xa_recv.at[i], dev_q(nbrs[n]))
+
+    def ra(j, n, zz):
+        view = pans[j].at[nbrs[n], a_range(1 + n), slab(zz)]
+        i = (j * 2 + n) * R + zz
+        return remote(view, view, ra_send.at[i], ra_recv.at[i], dev_q(nbrs[1 - n]))
+
+    def xb(j, n):
+        view = pans[j].at[q, b_range(0), slab(z)]
+        i = j * 2 + n
+        return remote(view, view, xb_send.at[i], xb_recv.at[i], dev_q(nbrs[n]))
+
+    def rb(j, n):
+        view = pans[j].at[nbrs[n], b_range(1 + n), slab(z)]
+        i = j * 2 + n
+        return remote(view, view, rb_send.at[i], rb_recv.at[i], dev_q(nbrs[1 - n]))
+
+    p = functools.partial
+
+    def gather_step(j, s):
+        if s == 0:
+            local(
+                j, panel_ref.at[:, :, panel_cols(k, j)],
+                pans[j].at[q, pl.ds(k * CB, CB), slab(z)],
+            ).wait()
+            pair_panel(j).wait_recv()
+            for up in (1, 0):
+                start(p(za, j, up, 1), z_send_cond(up, 1))
+            for n in (0, 1):
+                start(p(xb, j, n))
+            for n in (0, 1):
+                start(p(xa, j, n, z))
+            return
+        if s == 1:
+            for n in (0, 1):
+                xb(j, n).wait_recv()
+                start(p(rb, j, n))
+        if s == 2:
+            for n in (0, 1):
+                rb(j, n).wait_recv()
+            for up in (1, 0):
+                start(p(zb, j, up, 1), z_send_cond(up, 1))
+        if s < R:
+            for up in (1, 0):
+                cond = z_recv_cond(up, s)
+                when(cond, lambda: za(j, up, s).wait_recv())
+                if s < R - 1:
+                    start(p(za, j, up, s + 1), z_send_cond(up, s + 1))
+                for n in (0, 1):
+                    start(p(xa, j, n, z_from(up, s)), cond)
+        if 1 <= s <= R:
+            d = s - 1
+            for up in (1, 0) if d else (1,):
+                cond = z_recv_cond(up, d) if d else None
+                zz = z_from(up, d)
+                for n in (0, 1):
+                    when(cond, lambda: xa(j, n, zz).wait_recv())
+                    start(p(ra, j, n, zz), cond)
+        if s >= 3:
+            d = s - 2
+            for up in (1, 0):
+                when(z_recv_cond(up, d), lambda: zb(j, up, d).wait_recv())
+                if d < R - 1:
+                    start(p(zb, j, up, d + 1), z_send_cond(up, d + 1))
+        if s == steps - 1:
+            for zz in range(R):
+                for n in (0, 1):
+                    ra(j, n, zz).wait_recv()
+
+    steps = R + 2
+
+    def multiply(j, blocks, table, base):
+        pan = pans[j]
+
+        def turn(g, acc):
+            for u in range(UNROLL):
+                t = g * UNROLL + u
+                code = table[0, t]
+                slot = lax.rem(code, S)
+                col = lax.div(code, S)
+                product = jnp.dot(
+                    blocks[slot], pan[lax.div(col, group), lax.rem(col, group)],
+                    preferred_element_type=jnp.float32,
+                )
+                acc = jnp.where(table[1, t] == 1, 0.0, acc) + product
+                run[base + t] = acc
+            return acc
+
+        lax.fori_loop(0, S // UNROLL, turn, jnp.zeros((BS, width), jnp.float32))
+
+    def scatter(j, rel):
+        qq = (qx, qy, qd)[rel]
+        i = j * 3 + rel
+        return remote(
+            parts[j].at[pl.ds(qq * quarter, quarter)], arrives[j].at[rel],
+            rs_send.at[i], rs_recv.at[i], dev_q(qq),
+        )
+
+    def add_rows(j):
+        def row(i, carry):
+            a = own_table[2, i]
+            b = sib_table[2, i]
+            b = jnp.where(b > 0, b + S, 0)
+            parts[j][i] = run[a] + run[b]
+            return carry
+
+        lax.fori_loop(0, RB, row, 0)
+        for rel in (2, 0, 1):
+            start(p(scatter, j, rel))
+
+    def pair_rows(j):
+        return remote(sib_out.at[j], sib_in.at[j], out_send.at[j], out_recv.at[j], sib)
+
+    def square(j):
+        for rel in range(3):
+            scatter(j, rel).wait_recv()
+
+        def block(b, total, keep):
+            value = parts[j][q * quarter + b]
+            for rel in range(3):
+                value = value + arrives[j][rel, b]
+            value = value * value
+            keep(value)
+            return total + jnp.sum(value.reshape(BS // 8, 8, width), axis=0)
+
+        total = jnp.zeros((8, width), jnp.float32)
+        for i in range(own_rows):
+            def keep(value):
+                sib_out[j, i] = value
+            total = block((1 - k) * own_rows + i, total, keep)
+        start(p(pair_rows, j))
+        for i in range(own_rows):
+            def keep_mine(value):
+                mine[j, i] = value
+            total = block(k * own_rows + i, total, keep_mine)
+        stats[me, j] = total
+
+    lag = 2
+    for s in range(steps):
+        gather_step(0, s)
+        if s >= lag:
+            gather_step(1, s - lag)
+    local(2, table_ref, own_table).wait()
+    local(3, blocks_ref, own_blocks).wait()
+    pair_table().wait_recv()
+    local(4, sib_table_vmem, sib_table).start()
+    run[0] = jnp.zeros((BS, width), jnp.float32)
+    local(4, sib_table_vmem, sib_table).wait()
+    pair_blocks().wait_recv()
+    multiply(0, own_blocks, own_table, 1)
+    gather_step(1, steps - 2)
+    multiply(0, sib_blocks, sib_table, 1 + S)
+    add_rows(0)
+    gather_step(1, steps - 1)
+    multiply(1, own_blocks, own_table, 1)
+    multiply(1, sib_blocks, sib_table, 1 + S)
+    add_rows(1)
+    square(0)
+    square(1)
+
+    def stat(d):
+        t = lax.rem(me + d, total_devices)
+        return remote(
+            stats.at[me], stats.at[me], st_send.at[t], st_recv.at[me], (t // C, t % C)
+        )
+
+    def stat_from(d):
+        t = lax.rem(me + d, total_devices)
+        return remote(
+            stats.at[t], stats.at[t], st_send.at[t], st_recv.at[t], (t // C, t % C)
+        )
+
+    def send_stat(d, carry):
+        stat(d).start()
+        return carry
+
+    lax.fori_loop(1, total_devices, send_stat, 0)
+
+    def put(j, core, value_of):
+        for i in range(own_rows):
+            squares_ref[pl.ds(i * BS, BS), panel_cols(core, j)] = value_of(i)
+
+    for j in range(PARTS):
+        put(j, k, lambda i: mine[j, i])
+    for j in range(PARTS):
+        pair_rows(j).wait_recv()
+        put(j, 1 - k, lambda i: sib_in[j, i])
+
+    def take_stat(d, carry):
+        stat_from(d).wait_recv()
+        return carry
+
+    lax.fori_loop(1, total_devices, take_stat, 0)
+
+    def total_of(i, carry):
+        return carry[0] + stats[2 * i], carry[1] + stats[2 * i + 1]
+
+    zero = jnp.zeros((PARTS, 8, width), jnp.float32)
+    even, odd = lax.fori_loop(0, total_devices // 2, total_of, (zero, zero))
+    totals_ref[0] = even
+    totals_ref[1] = odd
+
+    for mk, cond in sent:
+        when(cond, lambda: mk().wait_send())
+
+    def done_stat(d, carry):
+        stat(d).wait_send()
+        return carry
+
+    lax.fori_loop(1, total_devices, done_stat, 0)
+
+
+def fused(blocks, owners, places, panel_matrix):
+    R = lax.axis_size("row")
+    C = lax.axis_size("col")
+    S, BS, _ = blocks.shape
+    CB, slab_rows, PW = panel_matrix.shape
+    RB = CB * C // R
+    width = PW // 2 // PARTS
+    group = 2 * CB
+    n_a = 10 * group // 16
+    quarter = RB // CHIPS
+    table = slot_table(owners, places, CB, RB)
+    dma = lambda n: pltpu.SemaphoreType.DMA((n,))
+    f32, bf16 = jnp.float32, blocks.dtype
+    cfg = (R, S, CB, RB, BS, width, n_a)
+    squares, totals = pl.pallas_call(
+        functools.partial(panel_kernel, cfg),
+        out_shape=(
+            jax.ShapeDtypeStruct((quarter // 2 * BS, PW), f32),
+            jax.ShapeDtypeStruct((2, PARTS, 8, width), f32),
+        ),
+        in_specs=[pl.BlockSpec(memory_space=pl.ANY)] * 3,
+        out_specs=[pl.BlockSpec(memory_space=pltpu.VMEM)] * 2,
+        scratch_shapes=[
+            pltpu.VMEM((CHIPS, group, BS, width), bf16),
+            pltpu.VMEM((CHIPS, group, BS, width), bf16),
+            pltpu.VMEM((S, BS, BS), bf16),
+            pltpu.VMEM((S, BS, BS), bf16),
+            pltpu.SMEM((8, 128), jnp.int32),
+            pltpu.SMEM((8, 128), jnp.int32),
+            pltpu.VMEM((8, 128), jnp.int32),
+            pltpu.VMEM((2 * S + 1, BS, width), f32),
+            pltpu.VMEM((RB, BS, width), f32),
+            pltpu.VMEM((RB, BS, width), f32),
+            pltpu.VMEM((3, quarter, BS, width), f32),
+            pltpu.VMEM((3, quarter, BS, width), f32),
+            pltpu.VMEM((PARTS, quarter // 2, BS, width), f32),
+            pltpu.VMEM((PARTS, quarter // 2, BS, width), f32),
+            pltpu.VMEM((PARTS, quarter // 2, BS, width), f32),
+            pltpu.VMEM((R * C, PARTS, 8, width), f32),
+            dma(5), dma(4), dma(4),
+            dma(PARTS * 2 * R), dma(PARTS * 2 * R), dma(PARTS * 2 * R), dma(PARTS * 2 * R),
+            dma(PARTS * 2 * R), dma(PARTS * 2 * R), dma(PARTS * 2 * R), dma(PARTS * 2 * R),
+            dma(PARTS * 2), dma(PARTS * 2), dma(PARTS * 2), dma(PARTS * 2),
+            dma(PARTS * 3), dma(PARTS * 3), dma(PARTS), dma(PARTS), dma(R * C), dma(R * C),
+        ],
+        compiler_params=pltpu.CompilerParams(
+            collective_id=0, has_side_effects=True, vmem_limit_bytes=48 << 20
+        ),
+        cost_estimate=pl.CostEstimate(
+            flops=2 * S * BS * BS * PW, bytes_accessed=4 << 20, transcendentals=0
+        ),
+    )(blocks, table, panel_matrix)
+    col_mean = jnp.sum(totals, axis=2).reshape(PW) / (CB * C * BS)
+    return squares / (col_mean + epsilon)
 
 
 def on_device(blocks, owners, places, panel_matrix):
@@ -63,6 +497,7 @@
 
 
 def solution(mesh):
+    fits = mesh.shape["col"] == 2 * CHIPS and mesh.shape["row"] == 4
     placed = (
         P(("row", "col"), None, None),
         P(("row", "col")),
@@ -70,5 +505,5 @@
         P("col", "row", None),
     )
     return jax.shard_map(
-        on_device, mesh=mesh, in_specs=placed, out_specs=P(("row", "col"), None), check_vma=False
+        fused if fits else on_device, mesh=mesh, in_specs=placed, out_specs=P(("row", "col"), None), check_vma=False
     )

time: 297 us -> 82 us (0.28)
  waiting for transfers between devices: 99.9 us -> 0 us
  Pallas kernels: 0 us -> 76.8 us
  other arithmetic: 78.5 us -> 2.26 us
  blocking collectives: 39.3 us -> 0 us
  matrix products: 27.9 us -> 0 us
  local copies, waits for them, and re-layouts: 27.2 us -> 2.57 us
  between operations: 13.4 us -> 0.07 us
  starting transfers between devices: 9.85 us -> 0 us
    pallas_call x0 -> x1, Pallas kernels: none -> 76.8 us  [fused(): pl.pallas_call(functools.partial(panel_kernel, cfg), out_shape=(jax.Shape...]
    scatter-add x4 -> x0, other arithmetic: 72.3 us -> none  [add_group(): return (partial_value.at[group_rows].add(product), None)]
    reduce_scatter x1 -> x0, waiting for transfers between devices: 52.1 us -> none  [on_device(): lax.psum_scatter(partial_rows, 'col', scatter_dimension=0, tiled=True)]
    psum x1 -> x0, blocking collectives: 39.3 us -> none  [on_device(): totals = lax.psum(jnp.sum(squares, axis=0), ('row', 'col'))]
    all_gather x1 -> x0, waiting for transfers between devices: 30 us -> none  [on_device(): panel_full = lax.all_gather(panel_matrix, 'row', axis=1, tiled=True)]
    dot_general x4 -> x0, matrix products: 27.9 us -> none  [add_group(): jnp.einsum('sab,sbp->sap', tile_group, pieces, preferred_element_type=jnp...]
    all_to_all x2 -> x0, waiting for transfers between devices: 17.1 us -> none  [the longest x1 17.1 us: on_device(): lax.all_to_all(outgoing, 'col', split_axis=0, concat_axis=0, tiled=True)]
    gather x4 -> x0, local copies, waits for them, and re-layouts: 11 us -> none  [add_group(): pieces = panel_full[group_cols]]
  transfers between devices with their start and end apart: 4 -> 0, of which waited for: 3 -> 0; matrix products, arithmetic and copies ran while one was open for 4% -> 0% of each run, Pallas kernels for 0% -> 0%
where the time goes in v1:
time: 82 us; the launch traced here: 81.7 us
  Pallas kernels  76.8 us (94%)
  local copies, waits for them, and re-layouts  2.57 us (3%)
  other arithmetic  2.26 us (3%)
    pallas_call x1, Pallas kernels, fused(): pl.pallas_call(functools.partial(panel_kernel, cfg), out_shape=(jax.Shape...  76.8 us
    unnamed x4, local copies, waits for them, and re-layouts  2.53 us

profile of v1, /device:TPU:0, one launch (start us, length us, event | category | flops | bytes accessed | tf_op | source)
XLA Modules:
  0.0 81.7 jit_solution(17472819383462910552)
XLA Ops:
  0.0 0.7 iota_add_fusion.1
  0.7 0.2 convert_reduce_fusion
  0.9 0.1 select_reduce_fusion
  1.0 0.1 slice_compare_fusion
  1.1 0.1 pad_add_fusion
  1.1 0.1 fusion
  1.3 0.1 convert_reduce_fusion.1
  1.5 0.0 copy-start
  1.5 1.6 %copy-done = bf16[64,128,128]{2,1,0:T(8,128)(2,1)S(1)} copy-done((bf16[64,128,128]{2,1,0:T(8,128)(2,1)S(1)}, bf16[64,128,128]{2,1,0:T(8,128)(2,1)}, u32[]{:S(2)}) %copy-start) | copy-done | bytes 2097176
  3.0 0.0 copy-start.1
  3.0 0.9 %copy-done.1 = bf16[8,32,512]{2,1,0:T(8,128)(2,1)S(1)} copy-done((bf16[8,32,512]{2,1,0:T(8,128)(2,1)S(1)}, bf16[8,32,512]{2,1,0:T(8,128)(2,1)}, u32[]{:S(2)}) %copy-start.1) | copy-done | bytes 262168
  4.0 76.8 %shard_map.46 = (f32[256,512]{1,0:T(8,128)S(1)}, f32[2,2,8,128]{3,2,1,0:T(8,128)S(1)}) custom-call(bf16[64,128,128]{2,1,0:T(8,128)(2,1)S(1)} %copy-done, s32[8,128]{1,0:T(8,128)S(1)} %stack.23.table_ref, bf16[8,32,512]{2,1,0:T(8,128)(2,1)S(1)} %copy-done.1), custom_call_target="tpu_custom_call" | custom-call | flops 1073741824 | bytes 4194304 | tf_op jit(solution)/shard_map/pallas_call | solution.py:401
  80.8 0.9 %broadcast_divide_fusion = f32[256,512]{1,0:T(8,128)} fusion(f32[256,512]{1,0:T(8,128)S(1)} %get-tuple-element.7, f32[512]{0:T(512)S(1)} %bitcast.7), kind=kLoop, calls=%fused_computation | loop fusion | flops 131072 | bytes 1050624 | tf_op jit(solution)/shard_map/div | solution.py:440
  (8 shorter events, 0.1 us)
Async XLA Ops:
  1.5 1.6 %copy-start = (bf16[64,128,128]{2,1,0:T(8,128)(2,1)S(1)}, bf16[64,128,128]{2,1,0:T(8,128)(2,1)}, u32[]{:S(2)}) copy-start(bf16[64,128,128]{2,1,0:T(8,128)(2,1)} %blocks_ref.1) | copy-start | bytes 6291460
  3.0 0.9 %copy-start.1 = (bf16[8,32,512]{2,1,0:T(8,128)(2,1)S(1)}, bf16[8,32,512]{2,1,0:T(8,128)(2,1)}, u32[]{:S(2)}) copy-start(bf16[8,32,512]{2,1,0:T(8,128)(2,1)} %panel_ref.1) | copy-start | bytes 786436

commit v2 on v1

--- a/solution.py
+++ b/solution.py
@@ -307,7 +307,7 @@
             def keep_mine(value):
                 mine[j, i] = value
             total = block(k * own_rows + i, total, keep_mine)
-        stats[me, j] = total
+        stats[me, pl.ds(j, 1)] = jnp.sum(total, axis=0, keepdims=True)
 
     lag = 2
     for s in range(steps):
@@ -369,7 +369,7 @@
     def total_of(i, carry):
         return carry[0] + stats[2 * i], carry[1] + stats[2 * i + 1]
 
-    zero = jnp.zeros((PARTS, 8, width), jnp.float32)
+    zero = jnp.zeros((PARTS, width), jnp.float32)
     even, odd = lax.fori_loop(0, total_devices // 2, total_of, (zero, zero))
     totals_ref[0] = even
     totals_ref[1] = odd
@@ -392,7 +392,7 @@
     RB = CB * C // R
     width = PW // 2 // PARTS
     group = 2 * CB
-    n_a = 10 * group // 16
+    n_a = 12 * group // 16
     quarter = RB // CHIPS
     table = slot_table(owners, places, CB, RB)
     dma = lambda n: pltpu.SemaphoreType.DMA((n,))
@@ -402,7 +402,7 @@
         functools.partial(panel_kernel, cfg),
         out_shape=(
             jax.ShapeDtypeStruct((quarter // 2 * BS, PW), f32),
-            jax.ShapeDtypeStruct((2, PARTS, 8, width), f32),
+            jax.ShapeDtypeStruct((2, PARTS, width), f32),
         ),
         in_specs=[pl.BlockSpec(memory_space=pl.ANY)] * 3,
         out_specs=[pl.BlockSpec(memory_space=pltpu.VMEM)] * 2,
@@ -422,7 +422,7 @@
             pltpu.VMEM((PARTS, quarter // 2, BS, width), f32),
             pltpu.VMEM((PARTS, quarter // 2, BS, width), f32),
             pltpu.VMEM((PARTS, quarter // 2, BS, width), f32),
-            pltpu.VMEM((R * C, PARTS, 8, width), f32),
+            pltpu.VMEM((R * C, PARTS, width), f32),
             dma(5), dma(4), dma(4),
             dma(PARTS * 2 * R), dma(PARTS * 2 * R), dma(PARTS * 2 * R), dma(PARTS * 2 * R),
             dma(PARTS * 2 * R), dma(PARTS * 2 * R), dma(PARTS * 2 * R), dma(PARTS * 2 * R),
@@ -430,13 +430,13 @@
             dma(PARTS * 3), dma(PARTS * 3), dma(PARTS), dma(PARTS), dma(R * C), dma(R * C),
         ],
         compiler_params=pltpu.CompilerParams(
-            collective_id=0, has_side_effects=True, vmem_limit_bytes=48 << 20
+            collective_id=0, has_side_effects=True, vmem_limit_bytes=60 << 20
         ),
         cost_estimate=pl.CostEstimate(
             flops=2 * S * BS * BS * PW, bytes_accessed=4 << 20, transcendentals=0
         ),
     )(blocks, table, panel_matrix)
-    col_mean = jnp.sum(totals, axis=2).reshape(PW) / (CB * C * BS)
+    col_mean = totals.reshape(PW) / (CB * C * BS)
     return squares / (col_mean + epsilon)
 
 

time: 82 us -> 76.8 us (0.937)
  Pallas kernels: 76.8 us -> 71.9 us
  local copies, waits for them, and re-layouts: 2.57 us -> 0.62 us
  other arithmetic: 2.26 us -> 3.96 us
    pallas_call x1, Pallas kernels: 76.8 us -> 71.9 us  [fused(): pl.pallas_call(functools.partial(panel_kernel, cfg), out_shape=(jax.Shape...]
    unnamed x4 -> x0, local copies, waits for them, and re-layouts: 2.53 us -> none
    div x1, other arithmetic: 0.86 us -> 1.9 us  [fused(): return squares / (col_mean + epsilon)]
where the time goes in v2:
time: 76.8 us; the launch traced here: 76.6 us
  Pallas kernels  71.9 us (94%)
  other arithmetic  3.96 us (5%)
    pallas_call x1, Pallas kernels, fused(): pl.pallas_call(functools.partial(panel_kernel, cfg), out_shape=(jax.Shape...  71.9 us
    div x1, other arithmetic, fused(): return squares / (col_mean + epsilon)  1.9 us

profile of v2, /device:TPU:0, one launch (start us, length us, event | category | flops | bytes accessed | tf_op | source)
XLA Modules:
  0.0 76.6 jit_solution(10405618913492721935)
XLA Ops:
  0.0 0.7 iota_add_fusion.1
  0.7 0.2 convert_reduce_fusion
  0.9 0.1 select_reduce_fusion
  1.0 0.1 slice_compare_fusion
  1.1 0.1 pad_add_fusion
  1.1 0.1 fusion
  1.3 0.1 convert_reduce_fusion.1
  1.4 0.6 stack.23.table_ref
  2.0 71.9 %shard_map.46 = (f32[256,512]{1,0:T(8,128)}, f32[2,2,128]{2,1,0:T(2,128)}) custom-call(bf16[64,128,128]{2,1,0:T(8,128)(2,1)} %blocks_ref.1, s32[8,128]{1,0:T(8,128)} %stack.23.table_ref, bf16[8,32,512]{2,1,0:T(8,128)(2,1)} %panel_ref.1), custom_call_target="tpu_custom_call" | custom-call | flops 1073741824 | bytes 4194304 | tf_op jit(solution)/shard_map/pallas_call | solution.py:401
  74.0 0.7 multiply_add_fusion
  74.7 1.9 %broadcast_divide_fusion = f32[256,512]{1,0:T(8,128)} fusion(f32[256,512]{1,0:T(8,128)} %get-tuple-element.7, f32[512]{0:T(512)S(1)} %bitcast.7), kind=kLoop, calls=%fused_computation | loop fusion | flops 131072 | bytes 1050624 | tf_op jit(solution)/shard_map/div | solution.py:440
  (5 shorter events, 0.0 us)

commit v3 on v2

--- a/solution.py
+++ b/solution.py
@@ -11,6 +11,8 @@
 CHIPS = 4
 PARTS = 2
 UNROLL = 8
+LEVELS = 32767.0
+smallest = 1e-30
 MESH = pl.DeviceIdType.MESH
 
 
@@ -40,12 +42,12 @@
     blocks_ref, table_ref, panel_ref,
     squares_ref, totals_ref,
     pan0, pan1, own_blocks, sib_blocks, own_table, sib_table, sib_table_vmem,
-    run, part0, part1, arrive0, arrive1, sib_in, sib_out, mine, stats,
+    run, part, code0, code1, arrive0, arrive1, scale_out, scale_in, sib_in, sib_out, mine, stats,
     local_sem, pair_send, pair_recv,
     za_send, za_recv, zb_send, zb_recv,
     xa_send, xa_recv, ra_send, ra_recv,
     xb_send, xb_recv, rb_send, rb_recv,
-    rs_send, rs_recv, out_send, out_recv, st_send, st_recv,
+    rs_send, rs_recv, sc_send, sc_recv, out_send, out_recv, st_send, st_recv,
 ):
     R, S, CB, RB, BS, width, n_a = cfg
     C = 2 * CHIPS
@@ -53,7 +55,7 @@
     group = 2 * CB
     quarter = RB // CHIPS
     own_rows = quarter // 2
-    pans, parts, arrives = (pan0, pan1), (part0, part1), (arrive0, arrive1)
+    pans, codes, arrives = (pan0, pan1), (code0, code1), (arrive0, arrive1)
     z = lax.axis_index("row")
     c = lax.axis_index("col")
     q = c // 2
@@ -262,37 +264,53 @@
 
         lax.fori_loop(0, S // UNROLL, turn, jnp.zeros((BS, width), jnp.float32))
 
+    others = (qx, qy, qd)
+
     def scatter(j, rel):
-        qq = (qx, qy, qd)[rel]
         i = j * 3 + rel
         return remote(
-            parts[j].at[pl.ds(qq * quarter, quarter)], arrives[j].at[rel],
-            rs_send.at[i], rs_recv.at[i], dev_q(qq),
+            codes[j].at[rel], arrives[j].at[rel], rs_send.at[i], rs_recv.at[i],
+            dev_q(others[rel]),
         )
 
+    def scatter_scale(j, rel):
+        i = j * 3 + rel
+        return remote(
+            scale_out.at[i], scale_in.at[i], sc_send.at[i], sc_recv.at[i], dev_q(others[rel])
+        )
+
+    def row_sum(i):
+        a = own_table[2, i]
+        b = sib_table[2, i]
+        b = jnp.where(b > 0, b + S, 0)
+        return run[a] + run[b]
+
     def add_rows(j):
-        def row(i, carry):
-            a = own_table[2, i]
-            b = sib_table[2, i]
-            b = jnp.where(b > 0, b + S, 0)
-            parts[j][i] = run[a] + run[b]
-            return carry
-
-        lax.fori_loop(0, RB, row, 0)
         for rel in (2, 0, 1):
+            for b in range(quarter):
+                value = row_sum(others[rel] * quarter + b)
+                top = jnp.max(jnp.abs(value), axis=0, keepdims=True)
+                top = jnp.maximum(top, smallest)
+                codes[j][rel, b] = jnp.round(value * (LEVELS / top)).astype(jnp.int32).astype(jnp.int16)
+                scale_out[j * 3 + rel, pl.ds(b, 1)] = top * (1.0 / LEVELS)
+            start(p(scatter_scale, j, rel))
             start(p(scatter, j, rel))
+        for b in range(quarter):
+            part[j, b] = row_sum(q * quarter + b)
 
     def pair_rows(j):
         return remote(sib_out.at[j], sib_in.at[j], out_send.at[j], out_recv.at[j], sib)
 
     def square(j):
         for rel in range(3):
+            scatter_scale(j, rel).wait_recv()
             scatter(j, rel).wait_recv()
 
         def block(b, total, keep):
-            value = parts[j][q * quarter + b]
+            value = part[j, b]
             for rel in range(3):
-                value = value + arrives[j][rel, b]
+                code = arrives[j][rel, b].astype(jnp.int32).astype(jnp.float32)
+                value = value + code * scale_in[j * 3 + rel, pl.ds(b, 1)]
             value = value * value
             keep(value)
             return total + jnp.sum(value.reshape(BS // 8, 8, width), axis=0)
@@ -415,10 +433,13 @@
             pltpu.SMEM((8, 128), jnp.int32),
             pltpu.VMEM((8, 128), jnp.int32),
             pltpu.VMEM((2 * S + 1, BS, width), f32),
-            pltpu.VMEM((RB, BS, width), f32),
-            pltpu.VMEM((RB, BS, width), f32),
-            pltpu.VMEM((3, quarter, BS, width), f32),
-            pltpu.VMEM((3, quarter, BS, width), f32),
+            pltpu.VMEM((PARTS, quarter, BS, width), f32),
+            pltpu.VMEM((3, quarter, BS, width), jnp.int16),
+            pltpu.VMEM((3, quarter, BS, width), jnp.int16),
+            pltpu.VMEM((3, quarter, BS, width), jnp.int16),
+            pltpu.VMEM((3, quarter, BS, width), jnp.int16),
+            pltpu.VMEM((PARTS * 3, quarter, width), f32),
+            pltpu.VMEM((PARTS * 3, quarter, width), f32),
             pltpu.VMEM((PARTS, quarter // 2, BS, width), f32),
             pltpu.VMEM((PARTS, quarter // 2, BS, width), f32),
             pltpu.VMEM((PARTS, quarter // 2, BS, width), f32),
@@ -427,7 +448,7 @@
             dma(PARTS * 2 * R), dma(PARTS * 2 * R), dma(PARTS * 2 * R), dma(PARTS * 2 * R),
             dma(PARTS * 2 * R), dma(PARTS * 2 * R), dma(PARTS * 2 * R), dma(PARTS * 2 * R),
             dma(PARTS * 2), dma(PARTS * 2), dma(PARTS * 2), dma(PARTS * 2),
-            dma(PARTS * 3), dma(PARTS * 3), dma(PARTS), dma(PARTS), dma(R * C), dma(R * C),
+            dma(PARTS * 3), dma(PARTS * 3), dma(PARTS * 3), dma(PARTS * 3), dma(PARTS), dma(PARTS), dma(R * C), dma(R * C),
         ],
         compiler_params=pltpu.CompilerParams(
             collective_id=0, has_side_effects=True, vmem_limit_bytes=60 << 20

time: 76.8 us -> 66.4 us (0.86)
  Pallas kernels: 71.9 us -> 61.5 us
    pallas_call x1, Pallas kernels: 71.9 us -> 61.5 us  [fused(): pl.pallas_call(functools.partial(panel_kernel, cfg), out_shape=(jax.Shape...]
where the time goes in v3:
time: 66.4 us; the launch traced here: 66.2 us
  Pallas kernels  61.5 us (93%)
  other arithmetic  3.96 us (6%)
    pallas_call x1, Pallas kernels, fused(): pl.pallas_call(functools.partial(panel_kernel, cfg), out_shape=(jax.Shape...  61.5 us
    div x1, other arithmetic, fused(): return squares / (col_mean + epsilon)  1.9 us

profile of v3, /device:TPU:0, one launch (start us, length us, event | category | flops | bytes accessed | tf_op | source)
XLA Modules:
  0.0 66.2 jit_solution(8940695474169128538)
XLA Ops:
  0.0 0.7 %iota_add_fusion.1 = (s32[64]{0:T(128)S(1)}, s32[64]{0:T(128)S(1)}, s32[64]{0:T(128)S(1)}) fusion(s32[64]{0:T(128)} %param.6, s32[64]{0:T(128)} %param.5), kind=kLoop, calls=%fused_computation.23 | loop fusion | flops 1600 | bytes 1280 | tf_op jit(solution)/shard_map/add | solution.py:24
  0.7 0.2 convert_reduce_fusion
  0.9 0.1 select_reduce_fusion
  1.0 0.1 slice_compare_fusion
  1.1 0.1 pad_add_fusion
  1.1 0.1 fusion
  1.3 0.1 convert_reduce_fusion.1
  1.4 0.6 stack.23.table_ref
  2.0 61.5 %shard_map.46 = (f32[256,512]{1,0:T(8,128)}, f32[2,2,128]{2,1,0:T(2,128)}) custom-call(bf16[64,128,128]{2,1,0:T(8,128)(2,1)} %blocks_ref.1, s32[8,128]{1,0:T(8,128)} %stack.23.table_ref, bf16[8,32,512]{2,1,0:T(8,128)(2,1)} %panel_ref.1), custom_call_target="tpu_custom_call" | custom-call | flops 1073741824 | bytes 4194304 | tf_op jit(solution)/shard_map/pallas_call | solution.py:419
  63.6 0.7 %multiply_add_fusion = f32[2,2,128]{2,1,0:T(2,128)S(1)} fusion(f32[2,2,128]{2,1,0:T(2,128)} %get-tuple-element.8), kind=kLoop, calls=%fused_computation.9 | loop fusion | flops 1024 | bytes 4096 | tf_op jit(solution)/shard_map/add | solution.py:461
  64.3 1.9 %broadcast_divide_fusion = f32[256,512]{1,0:T(8,128)} fusion(f32[256,512]{1,0:T(8,128)} %get-tuple-element.7, f32[512]{0:T(512)S(1)} %bitcast.7), kind=kLoop, calls=%fused_computation | loop fusion | flops 131072 | bytes 1050624 | tf_op jit(solution)/shard_map/div | solution.py:461
  (5 shorter events, 0.0 us)

commit v4 on v3

--- a/solution.py
+++ b/solution.py
@@ -21,18 +21,22 @@
     ids = jnp.arange(count, dtype=jnp.int32)
     rows = places // col_blocks
     cols = owners * col_blocks + places % col_blocks
-    key = rows * count + ids
-    rank = jnp.sum((key[None, :] < key[:, None]).astype(jnp.int32), axis=1)
-    chosen = (rank[None, :] == ids[:, None]).astype(jnp.int32)
-    code = jnp.sum(chosen * (cols * count + ids)[None, :], axis=1)
-    row_at = jnp.sum(chosen * rows[None, :], axis=1)
-    first = jnp.concatenate(
-        [jnp.ones((1,), jnp.int32), (row_at[1:] != row_at[:-1]).astype(jnp.int32)]
-    )
     targets = jnp.arange(row_blocks, dtype=jnp.int32)
-    upto = jnp.sum((rows[None, :] <= targets[:, None]).astype(jnp.int32), axis=1)
-    some = jnp.any(rows[None, :] == targets[:, None], axis=1)
-    last = jnp.where(some, upto, 0)
+    member = (rows[None, :] == targets[:, None]).astype(jnp.int32)
+    held = jnp.sum(member, axis=1)
+    filled = held + held % 2
+    below = (targets[None, :] < targets[:, None]).astype(jnp.int32)
+    base = jnp.sum(below * filled[None, :], axis=1)
+    earlier = jnp.logical_and(rows[None, :] == rows[:, None], ids[None, :] < ids[:, None])
+    rank = jnp.sum(earlier.astype(jnp.int32), axis=1)
+    at = rank + jnp.sum(member * base[:, None], axis=0)
+    entries = jnp.arange(count + row_blocks, dtype=jnp.int32)
+    chosen = (at[None, :] == entries[:, None]).astype(jnp.int32)
+    code = jnp.sum(chosen * (cols * 2 * count + ids - count)[None, :], axis=1) + count
+    pairs = entries[: entries.shape[0] // 2]
+    starts = jnp.logical_and(base[None, :] == 2 * pairs[:, None], held[None, :] > 0)
+    first = jnp.any(starts, axis=1).astype(jnp.int32)
+    last = jnp.where(held > 0, (base + filled) // 2, 0)
     lines = [jnp.pad(v, (0, 128 - v.shape[0])) for v in (code, first, last)]
     return jnp.stack(lines + [jnp.zeros((128,), jnp.int32)] * 5)
 
@@ -53,6 +57,7 @@
     C = 2 * CHIPS
     slab_rows = BS // R
     group = 2 * CB
+    pairs = (S + RB) // 2
     quarter = RB // CHIPS
     own_rows = quarter // 2
     pans, codes, arrives = (pan0, pan1), (code0, code1), (arrive0, arrive1)
@@ -110,7 +115,7 @@
             pans[j].at[q, pl.ds(k * CB, CB), slab(z)],
         ).start()
     local(2, table_ref, own_table).start()
-    local(3, blocks_ref, own_blocks).start()
+    local(3, blocks_ref, own_blocks.at[pl.ds(0, S)]).start()
     pl.semaphore_wait(barrier, total_devices - 1)
 
     sib = (z, q * 2 + 1 - k)
@@ -129,7 +134,7 @@
         return remote(table_ref, sib_table_vmem, pair_send.at[2], pair_recv.at[2], sib)
 
     def pair_blocks():
-        return remote(blocks_ref, sib_blocks, pair_send.at[3], pair_recv.at[3], sib)
+        return remote(blocks_ref, sib_blocks.at[pl.ds(0, S)], pair_send.at[3], pair_recv.at[3], sib)
 
     start(pair_table)
     start(pair_blocks)
@@ -251,18 +256,21 @@
         def turn(g, acc):
             for u in range(UNROLL):
                 t = g * UNROLL + u
-                code = table[0, t]
-                slot = lax.rem(code, S)
-                col = lax.div(code, S)
+                tiles, pieces = [], []
+                for e in (0, 1):
+                    code = table[0, 2 * t + e]
+                    col = lax.div(code, 2 * S)
+                    tiles.append(blocks[lax.rem(code, 2 * S)])
+                    pieces.append(pan[lax.div(col, group), lax.rem(col, group)])
                 product = jnp.dot(
-                    blocks[slot], pan[lax.div(col, group), lax.rem(col, group)],
+                    jnp.concatenate(tiles, axis=1), jnp.concatenate(pieces, axis=0),
                     preferred_element_type=jnp.float32,
                 )
                 acc = jnp.where(table[1, t] == 1, 0.0, acc) + product
                 run[base + t] = acc
             return acc
 
-        lax.fori_loop(0, S // UNROLL, turn, jnp.zeros((BS, width), jnp.float32))
+        lax.fori_loop(0, pairs // UNROLL, turn, jnp.zeros((BS, width), jnp.float32))
 
     others = (qx, qy, qd)
 
@@ -282,7 +290,7 @@
     def row_sum(i):
         a = own_table[2, i]
         b = sib_table[2, i]
-        b = jnp.where(b > 0, b + S, 0)
+        b = jnp.where(b > 0, b + pairs, 0)
         return run[a] + run[b]
 
     def add_rows(j):
@@ -333,19 +341,21 @@
         if s >= lag:
             gather_step(1, s - lag)
     local(2, table_ref, own_table).wait()
-    local(3, blocks_ref, own_blocks).wait()
+    local(3, blocks_ref, own_blocks.at[pl.ds(0, S)]).wait()
     pair_table().wait_recv()
     local(4, sib_table_vmem, sib_table).start()
     run[0] = jnp.zeros((BS, width), jnp.float32)
+    for held in (own_blocks, sib_blocks):
+        held[S] = jnp.zeros((BS, BS), held.dtype)
     local(4, sib_table_vmem, sib_table).wait()
     pair_blocks().wait_recv()
     multiply(0, own_blocks, own_table, 1)
     gather_step(1, steps - 2)
-    multiply(0, sib_blocks, sib_table, 1 + S)
+    multiply(0, sib_blocks, sib_table, 1 + pairs)
     add_rows(0)
     gather_step(1, steps - 1)
     multiply(1, own_blocks, own_table, 1)
-    multiply(1, sib_blocks, sib_table, 1 + S)
+    multiply(1, sib_blocks, sib_table, 1 + pairs)
     add_rows(1)
     square(0)
     square(1)
@@ -427,12 +437,12 @@
         scratch_shapes=[
             pltpu.VMEM((CHIPS, group, BS, width), bf16),
             pltpu.VMEM((CHIPS, group, BS, width), bf16),
-            pltpu.VMEM((S, BS, BS), bf16),
-            pltpu.VMEM((S, BS, BS), bf16),
+            pltpu.VMEM((S + 1, BS, BS), bf16),
+            pltpu.VMEM((S + 1, BS, BS), bf16),
             pltpu.SMEM((8, 128), jnp.int32),
             pltpu.SMEM((8, 128), jnp.int32),
             pltpu.VMEM((8, 128), jnp.int32),
-            pltpu.VMEM((2 * S + 1, BS, width), f32),
+            pltpu.VMEM((S + RB + 1, BS, width), f32),
             pltpu.VMEM((PARTS, quarter, BS, width), f32),
             pltpu.VMEM((3, quarter, BS, width), jnp.int16),
             pltpu.VMEM((3, quarter, BS, width), jnp.int16),

time: 66.4 us -> 66.1 us (level)
    select_n x1 -> x2, other arithmetic: 0.01 us -> 0.7 us  [the longest x1 0.68 us: slot_table(): rows = places // col_blocks]
where the time goes in v4:
time: 66.1 us; the launch traced here: 65.9 us
  Pallas kernels  61.2 us (93%)
  other arithmetic  4.03 us (6%)
    pallas_call x1, Pallas kernels, fused(): pl.pallas_call(functools.partial(panel_kernel, cfg), out_shape=(jax.Shape...  61.2 us
    div x1, other arithmetic, fused(): return squares / (col_mean + epsilon)  1.9 us

profile of v4, /device:TPU:0, one launch (start us, length us, event | category | flops | bytes accessed | tf_op | source)
XLA Modules:
  0.0 65.9 jit_solution(6724288348365609263)
XLA Ops:
  0.0 0.7 %and_select_fusion.3 = (s32[64]{0:T(128)S(1)}, s32[64]{0:T(128)S(1)}) fusion(s32[64]{0:T(128)} %param.6, s32[64]{0:T(128)} %param.5), kind=kLoop, calls=%fused_computation.19 | loop fusion | flops 1536 | bytes 1024 | tf_op jit(solution)/shard_map/jit(floor_divide)/jit(_where)/select_n | solution.py:22
  0.7 0.1 convert_reduce_fusion.1
  0.8 0.1 select_reduce_fusion.2
  0.9 0.1 and_reduce_fusion
  1.1 0.1 select_reduce_fusion.1
  1.2 0.2 convert_reduce_fusion
  1.3 0.1 select_reduce_fusion
  1.5 0.6 stack.23.table_ref
  2.1 61.2 %shard_map.46 = (f32[256,512]{1,0:T(8,128)}, f32[2,2,128]{2,1,0:T(2,128)}) custom-call(bf16[64,128,128]{2,1,0:T(8,128)(2,1)} %blocks_ref.1, s32[8,128]{1,0:T(8,128)} %stack.23.table_ref, bf16[8,32,512]{2,1,0:T(8,128)(2,1)} %panel_ref.1), custom_call_target="tpu_custom_call" | custom-call | flops 1073741824 | bytes 4194304 | tf_op jit(solution)/shard_map/pallas_call | solution.py:429
  63.3 0.7 %multiply_add_fusion = f32[2,2,128]{2,1,0:T(2,128)S(1)} fusion(f32[2,2,128]{2,1,0:T(2,128)} %get-tuple-element.8), kind=kLoop, calls=%fused_computation.14 | loop fusion | flops 1024 | bytes 4096 | tf_op jit(solution)/shard_map/add | solution.py:471
  64.0 1.9 %broadcast_divide_fusion = f32[256,512]{1,0:T(8,128)} fusion(f32[256,512]{1,0:T(8,128)} %get-tuple-element.7, f32[512]{0:T(512)S(1)} %bitcast.7), kind=kLoop, calls=%fused_computation | loop fusion | flops 131072 | bytes 1050624 | tf_op jit(solution)/shard_map/div | solution.py:471
  (11 shorter events, 0.1 us)

commit v5 on v4

--- a/solution.py
+++ b/solution.py
@@ -115,7 +115,6 @@
             pans[j].at[q, pl.ds(k * CB, CB), slab(z)],
         ).start()
     local(2, table_ref, own_table).start()
-    local(3, blocks_ref, own_blocks.at[pl.ds(0, S)]).start()
     pl.semaphore_wait(barrier, total_devices - 1)
 
     sib = (z, q * 2 + 1 - k)
@@ -137,7 +136,6 @@
         return remote(blocks_ref, sib_blocks.at[pl.ds(0, S)], pair_send.at[3], pair_recv.at[3], sib)
 
     start(pair_table)
-    start(pair_blocks)
 
     def dev_q(qq):
         return (z, qq * 2 + k)
@@ -340,6 +338,9 @@
         gather_step(0, s)
         if s >= lag:
             gather_step(1, s - lag)
+        if s == lag:
+            start(pair_blocks)
+            local(3, blocks_ref, own_blocks.at[pl.ds(0, S)]).start()
     local(2, table_ref, own_table).wait()
     local(3, blocks_ref, own_blocks.at[pl.ds(0, S)]).wait()
     pair_table().wait_recv()
@@ -420,7 +421,7 @@
     RB = CB * C // R
     width = PW // 2 // PARTS
     group = 2 * CB
-    n_a = 12 * group // 16
+    n_a = 11 * group // 16
     quarter = RB // CHIPS
     table = slot_table(owners, places, CB, RB)
     dma = lambda n: pltpu.SemaphoreType.DMA((n,))

time: 66.1 us -> 68 us (1.029)
  Pallas kernels: 61.2 us -> 63.1 us
    pallas_call x1, Pallas kernels: 61.2 us -> 63.1 us  [fused(): pl.pallas_call(functools.partial(panel_kernel, cfg), out_shape=(jax.Shape...]
where the time goes in v5:
time: 68 us; the launch traced here: 67.8 us
  Pallas kernels  63.1 us (93%)
  other arithmetic  4.03 us (6%)
    pallas_call x1, Pallas kernels, fused(): pl.pallas_call(functools.partial(panel_kernel, cfg), out_shape=(jax.Shape...  63.1 us
    div x1, other arithmetic, fused(): return squares / (col_mean + epsilon)  1.9 us

profile of v5, /device:TPU:0, one launch (start us, length us, event | category | flops | bytes accessed | tf_op | source)
XLA Modules:
  0.0 67.8 jit_solution(14359734710268324759)
XLA Ops:
  0.0 0.7 %and_select_fusion.3 = (s32[64]{0:T(128)S(1)}, s32[64]{0:T(128)S(1)}) fusion(s32[64]{0:T(128)} %param.6, s32[64]{0:T(128)} %param.5), kind=kLoop, calls=%fused_computation.19 | loop fusion | flops 1536 | bytes 1024 | tf_op jit(solution)/shard_map/jit(floor_divide)/jit(_where)/select_n | solution.py:22
  0.7 0.1 convert_reduce_fusion.1
  0.8 0.1 select_reduce_fusion.2
  0.9 0.1 and_reduce_fusion
  1.1 0.1 select_reduce_fusion.1
  1.2 0.2 convert_reduce_fusion
  1.3 0.1 select_reduce_fusion
  1.5 0.6 stack.23.table_ref
  2.1 63.1 %shard_map.46 = (f32[256,512]{1,0:T(8,128)}, f32[2,2,128]{2,1,0:T(2,128)}) custom-call(bf16[64,128,128]{2,1,0:T(8,128)(2,1)} %blocks_ref.1, s32[8,128]{1,0:T(8,128)} %stack.23.table_ref, bf16[8,32,512]{2,1,0:T(8,128)(2,1)} %panel_ref.1), custom_call_target="tpu_custom_call" | custom-call | flops 1073741824 | bytes 4194304 | tf_op jit(solution)/shard_map/pallas_call | solution.py:430
  65.2 0.7 %multiply_add_fusion = f32[2,2,128]{2,1,0:T(2,128)S(1)} fusion(f32[2,2,128]{2,1,0:T(2,128)} %get-tuple-element.8), kind=kLoop, calls=%fused_computation.14 | loop fusion | flops 1024 | bytes 4096 | tf_op jit(solution)/shard_map/add | solution.py:472
  65.9 1.9 %broadcast_divide_fusion = f32[256,512]{1,0:T(8,128)} fusion(f32[256,512]{1,0:T(8,128)} %get-tuple-element.7, f32[512]{0:T(512)S(1)} %bitcast.7), kind=kLoop, calls=%fused_computation | loop fusion | flops 131072 | bytes 1050624 | tf_op jit(solution)/shard_map/div | solution.py:472
  (11 shorter events, 0.1 us)

commit v6 on v4

--- a/solution.py
+++ b/solution.py
@@ -420,7 +420,7 @@
     RB = CB * C // R
     width = PW // 2 // PARTS
     group = 2 * CB
-    n_a = 12 * group // 16
+    n_a = 14 * group // 16
     quarter = RB // CHIPS
     table = slot_table(owners, places, CB, RB)
     dma = lambda n: pltpu.SemaphoreType.DMA((n,))

time: 66.1 us -> 68.2 us (1.032)
  Pallas kernels: 61.2 us -> 63.4 us
    pallas_call x1, Pallas kernels: 61.2 us -> 63.4 us  [fused(): pl.pallas_call(functools.partial(panel_kernel, cfg), out_shape=(jax.Shape...]
where the time goes in v6:
time: 68.2 us; the launch traced here: 68.1 us
  Pallas kernels  63.4 us (93%)
  other arithmetic  4.03 us (6%)
    pallas_call x1, Pallas kernels, fused(): pl.pallas_call(functools.partial(panel_kernel, cfg), out_shape=(jax.Shape...  63.4 us
    div x1, other arithmetic, fused(): return squares / (col_mean + epsilon)  1.9 us

profile of v6, /device:TPU:0, one launch (start us, length us, event | category | flops | bytes accessed | tf_op | source)
XLA Modules:
  0.0 68.1 jit_solution(4238919134290039934)
XLA Ops:
  0.0 0.7 %and_select_fusion.3 = (s32[64]{0:T(128)S(1)}, s32[64]{0:T(128)S(1)}) fusion(s32[64]{0:T(128)} %param.6, s32[64]{0:T(128)} %param.5), kind=kLoop, calls=%fused_computation.19 | loop fusion | flops 1536 | bytes 1024 | tf_op jit(solution)/shard_map/jit(floor_divide)/jit(_where)/select_n | solution.py:22
  0.7 0.1 convert_reduce_fusion.1
  0.8 0.1 select_reduce_fusion.2
  0.9 0.1 and_reduce_fusion
  1.1 0.1 select_reduce_fusion.1
  1.2 0.2 convert_reduce_fusion
  1.3 0.1 select_reduce_fusion
  1.5 0.6 stack.23.table_ref
  2.1 63.4 %shard_map.46 = (f32[256,512]{1,0:T(8,128)}, f32[2,2,128]{2,1,0:T(2,128)}) custom-call(bf16[64,128,128]{2,1,0:T(8,128)(2,1)} %blocks_ref.1, s32[8,128]{1,0:T(8,128)} %stack.23.table_ref, bf16[8,32,512]{2,1,0:T(8,128)(2,1)} %panel_ref.1), custom_call_target="tpu_custom_call" | custom-call | flops 1073741824 | bytes 4194304 | tf_op jit(solution)/shard_map/pallas_call | solution.py:429
  65.5 0.7 %multiply_add_fusion = f32[2,2,128]{2,1,0:T(2,128)S(1)} fusion(f32[2,2,128]{2,1,0:T(2,128)} %get-tuple-element.8), kind=kLoop, calls=%fused_computation.14 | loop fusion | flops 1024 | bytes 4096 | tf_op jit(solution)/shard_map/add | solution.py:471
  66.2 1.9 %broadcast_divide_fusion = f32[256,512]{1,0:T(8,128)} fusion(f32[256,512]{1,0:T(8,128)} %get-tuple-element.7, f32[512]{0:T(512)S(1)} %bitcast.7), kind=kLoop, calls=%fused_computation | loop fusion | flops 131072 | bytes 1050624 | tf_op jit(solution)/shard_map/div | solution.py:471
  (11 shorter events, 0.1 us)

commit v7 on v5

--- a/solution.py
+++ b/solution.py
@@ -421,7 +421,7 @@
     RB = CB * C // R
     width = PW // 2 // PARTS
     group = 2 * CB
-    n_a = 11 * group // 16
+    n_a = 12 * group // 16
     quarter = RB // CHIPS
     table = slot_table(owners, places, CB, RB)
     dma = lambda n: pltpu.SemaphoreType.DMA((n,))

time: 68 us -> 66.1 us (0.972)
  Pallas kernels: 63.1 us -> 61.2 us
    pallas_call x1, Pallas kernels: 63.1 us -> 61.2 us  [fused(): pl.pallas_call(functools.partial(panel_kernel, cfg), out_shape=(jax.Shape...]
where the time goes in v7:
time: 66.1 us; the launch traced here: 65.9 us
  Pallas kernels  61.2 us (93%)
  other arithmetic  4.03 us (6%)
    pallas_call x1, Pallas kernels, fused(): pl.pallas_call(functools.partial(panel_kernel, cfg), out_shape=(jax.Shape...  61.2 us
    div x1, other arithmetic, fused(): return squares / (col_mean + epsilon)  1.9 us

profile of v7, /device:TPU:0, one launch (start us, length us, event | category | flops | bytes accessed | tf_op | source)
XLA Modules:
  0.0 65.9 jit_solution(18304684671752804554)
XLA Ops:
  0.0 0.7 %and_select_fusion.3 = (s32[64]{0:T(128)S(1)}, s32[64]{0:T(128)S(1)}) fusion(s32[64]{0:T(128)} %param.6, s32[64]{0:T(128)} %param.5), kind=kLoop, calls=%fused_computation.19 | loop fusion | flops 1536 | bytes 1024 | tf_op jit(solution)/shard_map/jit(floor_divide)/jit(_where)/select_n | solution.py:22
  0.7 0.1 convert_reduce_fusion.1
  0.8 0.1 select_reduce_fusion.2
  0.9 0.1 and_reduce_fusion
  1.1 0.1 select_reduce_fusion.1
  1.2 0.2 convert_reduce_fusion
  1.3 0.1 select_reduce_fusion
  1.5 0.6 stack.23.table_ref
  2.1 61.2 %shard_map.46 = (f32[256,512]{1,0:T(8,128)}, f32[2,2,128]{2,1,0:T(2,128)}) custom-call(bf16[64,128,128]{2,1,0:T(8,128)(2,1)} %blocks_ref.1, s32[8,128]{1,0:T(8,128)} %stack.23.table_ref, bf16[8,32,512]{2,1,0:T(8,128)(2,1)} %panel_ref.1), custom_call_target="tpu_custom_call" | custom-call | flops 1073741824 | bytes 4194304 | tf_op jit(solution)/shard_map/pallas_call | solution.py:430
  63.3 0.7 %multiply_add_fusion = f32[2,2,128]{2,1,0:T(2,128)S(1)} fusion(f32[2,2,128]{2,1,0:T(2,128)} %get-tuple-element.8), kind=kLoop, calls=%fused_computation.14 | loop fusion | flops 1024 | bytes 4096 | tf_op jit(solution)/shard_map/add | solution.py:472
  64.0 1.9 %broadcast_divide_fusion = f32[256,512]{1,0:T(8,128)} fusion(f32[256,512]{1,0:T(8,128)} %get-tuple-element.7, f32[512]{0:T(512)S(1)} %bitcast.7), kind=kLoop, calls=%fused_computation | loop fusion | flops 131072 | bytes 1050624 | tf_op jit(solution)/shard_map/div | solution.py:472
  (11 shorter events, 0.1 us)
